TPU v7x, 1024 devices: a whole 4x8x16 slice. The times are simulated.
1024 devices in a mesh: gx: 16 (over z), gy: 4 (over x_hi, core), gz: 16 (over x_lo, y).
Axes of the slice: x: 4 (x_hi: 2, x_lo: 2; x = x_hi * 2 + x_lo), y: 8, z: 16, core: 2. Of those that a mesh axis runs over, the one named last changes fastest.
Arguments:
- species: float32 [128, 32, 128, 256], P('gx', 'gy', 'gz'), may hold values from 0.25 to 4
- substeps: int32 [64, 4, 16], P('gx', 'gy', 'gz'), may hold values from 1 to 4, as said below
- reactants: int32 [1024, 256], replicated, may hold values from 0 to 2, as said below
- products: int32 [1024, 256], replicated, may hold values from 0 to 2, as said below
- rate_const: float32 [1024], replicated, may hold values from 0.01 to 0.2
- velocity: float32 [3, 128, 32, 128], P(None, 'gx', 'gy', 'gz'), may hold values from -0.3 to 0.3
- viscosity: float32 [128, 32, 128], P('gx', 'gy', 'gz'), may hold values from 0.25 to 1
- diffusivity: float32 [256], replicated, may hold values from 0.03 to 0.12
Outputs:
- evolved: float32 [128, 32, 128, 256], P('gx', 'gy', 'gz')
Inputs may be any that keep to these rules, and one draw needn't show every extreme that they name: `substeps`: one entry for each block of 128 cells (2 x-planes of a brick); the value 4 occurs in every draw. `reactants`: each row sums to 2. `products`: each row sums to 2.
All inputs are finite; a program needn't handle non-finite values.
Results may differ from a plain program's by a relative error of at most 0.00077.
Values sent between devices are 32-bit elements; how exact they have to be, the bound alone decides.
A program may use at most 32 MiB of HBM per device.

v0:
```python
import jax
import jax.numpy as jnp
from jax import lax
from jax.sharding import PartitionSpec as P

BLOCK = 128
MAX_SUB = 4


def with_halo(value, sides, width):
    for axis, dim in sides:
        peers, length = (lax.axis_size(axis), value.shape[dim])
        up = [(i, (i + 1) % peers) for i in range(peers)]
        down = [(j, i) for i, j in up]
        last = lax.slice_in_dim(value, length - width, length, axis=dim)
        initial = lax.slice_in_dim(value, 0, width, axis=dim)
        before = lax.ppermute(last, axis, up)
        after = lax.ppermute(initial, axis, down)
        value = jnp.concatenate([before, value, after], axis=dim)
    return value


def react(conc, length, reactant_table, stoich, rate_const):
    logs = jnp.log(conc)
    expo = lax.dot_general(
        logs,
        reactant_table,
        (((1,), (1,)), ((), ())),
        precision=lax.Precision.HIGHEST,
        preferred_element_type=jnp.float32,
    )
    rates = (rate_const * jnp.exp(expo)).astype(jnp.bfloat16)
    terms = jnp.dot(rates, stoich, preferred_element_type=jnp.float32)
    width = conc.shape[1]
    made = terms[:, :width]
    used = terms[:, width:]
    return conc * (conc + length * made) / (conc + length * used)


def integrate(rows, counts, reactant_table, stoich, rate_const):
    order = jnp.argsort(-counts)
    sorted_rows = rows[order]
    sorted_counts = counts[order]
    length = 1.0 / sorted_counts.astype(jnp.float32)[:, None]
    for level in range(1, MAX_SUB + 1):
        live = jnp.sum((sorted_counts >= level).astype(jnp.int32))
        trips = (live + BLOCK - 1) // BLOCK

        def tile_step(tile, state, level=level):
            start = tile * BLOCK
            block = lax.dynamic_slice_in_dim(state, start, BLOCK, 0)
            tile_length = lax.dynamic_slice_in_dim(length, start, BLOCK, 0)
            tile_counts = lax.dynamic_slice_in_dim(sorted_counts, start, BLOCK, 0)
            fresh = react(block, tile_length, reactant_table, stoich, rate_const)
            kept = jnp.where((tile_counts >= level)[:, None], fresh, block)
            return lax.dynamic_update_slice_in_dim(state, kept, start, 0)

        sorted_rows = lax.fori_loop(0, trips, tile_step, sorted_rows)
    inverse = jnp.argsort(order)
    return sorted_rows[inverse]


def window(array, axis, offset):
    index = []
    for place in range(3):
        shift = offset if place == axis else 0
        index.append(slice(1 + shift, array.shape[place] - 1 + shift))
    return array[tuple(index)]


def divergence(field, coef, diffusivity):
    inner = window(field, 0, 0)
    visc = window(coef[3], 0, 0)
    total = jnp.zeros(inner.shape, jnp.float32)
    for axis in range(3):
        ahead = window(field, axis, 1)
        behind = window(field, axis, -1)
        speed = window(coef[axis], 0, 0)[..., None]
        speed_behind = window(coef[axis], axis, -1)[..., None]
        visc_ahead = window(coef[3], axis, 1)
        visc_behind = window(coef[3], axis, -1)
        flux_up = speed * (inner + ahead) * 0.5 - diffusivity * ((visc + visc_ahead) * 0.5)[
            ..., None
        ] * (ahead - inner)
        flux_down = speed_behind * (behind + inner) * 0.5 - diffusivity * (
            (visc_behind + visc) * 0.5
        )[..., None] * (inner - behind)
        total = total - (flux_up - flux_down)
    return total


def shards(species, substeps, reactants, products, rate_const, velocity, viscosity, diffusivity):
    cells_x, cells_y, cells_z, width = species.shape
    reactant_table = reactants.astype(jnp.float32)
    stoich = jnp.concatenate([products, reactants], axis=1).astype(jnp.bfloat16)
    rows = species.reshape(-1, width)
    cell_counts = jnp.repeat(substeps.reshape(-1), BLOCK)
    rows = integrate(rows, cell_counts, reactant_table, stoich, rate_const)
    field = rows.reshape(cells_x, cells_y, cells_z, width)
    coef = jnp.concatenate([velocity, viscosity[None]], axis=0)
    coef_pad = with_halo(coef, (("gx", 1), ("gy", 2), ("gz", 3)), 1)

    def advance(state):
        padded = with_halo(state, (("gx", 0), ("gy", 1), ("gz", 2)), 1)
        return state + divergence(padded, coef_pad, diffusivity)

    second = advance(advance(field))
    return 0.5 * field + 0.5 * second


def solution(mesh):
    return jax.shard_map(
        shards,
        mesh=mesh,
        in_specs=(
            P("gx", "gy", "gz", None),
            P("gx", "gy", "gz"),
            P(),
            P(),
            P(),
            P(None, "gx", "gy", "gz"),
            P("gx", "gy", "gz"),
            P(),
        ),
        out_specs=P("gx", "gy", "gz", None),
        check_vma=False,
    )
```

profile of v0, /device:TPU:1, one launch (start us, length us, event | category | flops | bytes accessed | tf_op | source)
XLA Modules:
  0.0 142.7 jit_solution(11457780070861557395)
XLA Ops:
  0.8 18.8 %collective-permute-start.1 = (f32[4,1,8,8]{3,2,1,0:T(8,128)S(1)}, f32[4,1,8,8]{3,2,1,0:T(8,128)S(1)}, u32[]{:S(2)}, u32[]{:S(2)}) collective-permute-start(f32[4,1,8,8]{3,2,1,0:T(8,128)S(1)} %get-tuple-element.276), channel_id=1, source_target_pairs={{64,0},{128,64},{192,128},{256,192},{320,256},{384,320},{448,384},... | collective-permute-start | bytes 3080 | tf_op jit(solution)/shard_map/ppermute | solution.py:18
  23.0 3.8 %sort.31 = (s32[512]{0:T(512)}, s32[512]{0:T(512)S(1)}) sort(s32[512]{0:T(512)S(1)} %bitcast_negate_fusion, s32[512]{0:T(512)S(1)} %iota.7), dimensions={0}, to_apply=%region_0.0 | sort | flops 4608 | bytes 8192 | tf_op jit(solution)/shard_map/jit(argsort)/sort | solution.py:41
  26.8 3.5 %gather_fusion.1 = s32[512]{0:T(512)S(1)} fusion(s32[512]{0:T(512)S(1)} %broadcast_bitcast_fusion, s32[1024]{0:T(1024)S(1)} %pad_clamp_fusion.1), kind=kCustom, calls=%fused_computation.1 | custom fusion | bytes 6144 | tf_op jit(solution)/shard_map/gather | solution.py:43
  38.7 7.1 %while.40 = (s32[]{:T(128)}, f32[512,256]{1,0:T(8,128)S(1)}, s32[]{:T(128)}, s32[512]{0:T(512)S(1)}, f32[512,1]{0,1:T(1,128)S(1)}, /*index=5*/f32[1024]{0:T(1024...) while((s32[]{:T(128)}, f32[512,256]{1,0:T(8,128)S(1)}, ...), condition=%wide.region_3.4_spmd, body=%wide.region_2.3_spmd.sunk | while | flops 537362560 | bytes 3545915 | solution.py:58
  45.8 3.6 %while.41 = (s32[]{:T(128)}, f32[512,256]{1,0:T(8,128)S(1)}, s32[]{:T(128)}, s32[512]{0:T(512)S(1)}, f32[512,1]{0,1:T(1,128)S(1)}, /*index=5*/f32[1024]{0:T(1024...) while((s32[]{:T(128)}, f32[512,256]{1,0:T(8,128)S(1)}, ...), condition=%wide.region_6.7_spmd, body=%wide.region_5.6_spmd.sunk | while | flops 537362560 | bytes 3545915 | solution.py:58
  49.5 3.8 %sort.32 = (s32[512]{0:T(512)}, s32[512]{0:T(512)S(1)}) sort(s32[512]{0:T(512)S(1)} %get-tuple-element.179, s32[512]{0:T(512)S(1)} %iota.8), dimensions={0}, to_apply=%region_13.14 | sort | flops 4608 | bytes 8192 | tf_op jit(solution)/shard_map/jit(argsort)/sort | solution.py:59
  53.3 4.6 %collective-permute-start.3 = (f32[4,10,1,8]{3,2,1,0:T(1,128)S(1)}, f32[4,10,1,8]{3,2,1,0:T(1,128)S(1)}, u32[]{:S(2)}, u32[]{:S(2)}) collective-permute-start(f32[4,10,1,8]{3,2,1,0:T(1,128)S(1)} %get-tuple-element.274), channel_id=1, source_target_pairs={{16,0},{32,16},{48,32},{0,48},{17,1},{33,17},{49,33},{1,49},{18,2}... | collective-permute-start | bytes 3848 | tf_op jit(solution)/shard_map/ppermute | solution.py:18
  58.0 2.8 %collective-permute-start.2 = (f32[4,10,1,8]{3,2,1,0:T(1,128)S(1)}, f32[4,10,1,8]{3,2,1,0:T(1,128)S(1)}, u32[]{:S(2)}, u32[]{:S(2)}) collective-permute-start(f32[4,10,1,8]{3,2,1,0:T(1,128)S(1)} %get-tuple-element.273), channel_id=1, source_target_pairs={{0,16},{16,32},{32,48},{48,0},{1,17},{17,33},{33,49},{49,1},{2,18}... | collective-permute-start | bytes 3848 | tf_op jit(solution)/shard_map/ppermute | solution.py:17
  62.6 9.2 %collective-permute-start.5 = (f32[4,10,10,1]{3,2,1,0:T(8,128)S(1)}, f32[4,10,10,1]{3,2,1,0:T(8,128)S(1)}, u32[]{:S(2)}, u32[]{:S(2)}) collective-permute-start(f32[4,10,10,1]{3,2,1,0:T(8,128)S(1)} %get-tuple-element.272), channel_id=1, source_target_pairs={{1,0},{2,1},{3,2},{4,3},{5,4},{6,5},{7,6},{8,7},{9,8},{10,9},{11,1... | collective-permute-start | bytes 4808 | tf_op jit(solution)/shard_map/ppermute | solution.py:18
  73.8 2.5 %collective-permute-start.6 = (f32[1,8,8,256]{3,2,1,0:T(8,128)S(1)}, f32[1,8,8,256]{3,2,1,0:T(8,128)S(1)}, u32[]{:S(2)}, u32[]{:S(2)}) collective-permute-start(f32[1,8,8,256]{3,2,1,0:T(8,128)S(1)} %get-tuple-element.266), channel_id=1, source_target_pairs={{64,0},{128,64},{192,128},{256,192},{320,256},{384,320},{448,384},... | collective-permute-start | bytes 196616 | tf_op jit(solution)/shard_map/ppermute | solution.py:18
  76.3 3.3 %collective-permute-start.7 = (f32[1,8,8,256]{3,2,1,0:T(8,128)S(1)}, f32[1,8,8,256]{3,2,1,0:T(8,128)S(1)}, u32[]{:S(2)}, u32[]{:S(2)}) collective-permute-start(f32[1,8,8,256]{3,2,1,0:T(8,128)S(1)} %get-tuple-element.265), channel_id=1, source_target_pairs={{0,64},{64,128},{128,192},{192,256},{256,320},{320,384},{384,448},... | collective-permute-start | bytes 196616 | tf_op jit(solution)/shard_map/ppermute | solution.py:17
  79.6 5.5 %collective-permute-done.4 = f32[4,10,10,1]{3,2,1,0:T(8,128)S(1)} collective-permute-done((f32[4,10,10,1]{3,2,1,0:T(8,128)S(1)}, f32[4,10,10,1]{3,2,1,0:T(8,128)S(1)}, u32[]{:S(2)}, u32[]{:S(2)}) %collective-permute-start.4) | collective-permute-done | bytes 1632 | tf_op jit(solution)/shard_map/ppermute | solution.py:17
  85.5 4.4 %collective-permute-start.9 = (f32[10,1,8,256]{3,2,1,0:T(8,128)S(1)}, f32[10,1,8,256]{3,2,1,0:T(8,128)S(1)}, u32[]{:S(2)}, u32[]{:S(2)}) collective-permute-start(f32[10,1,8,256]{3,2,1,0:T(8,128)S(1)} %get-tuple-element.262), channel_id=1, source_target_pairs={{0,16},{16,32},{32,48},{48,0},{1,17},{17,33},{33,49},{49,1},{2,18}... | collective-permute-start | bytes 245768 | tf_op jit(solution)/shard_map/ppermute | solution.py:17
  92.0 5.2 %collective-permute-done.8 = f32[10,1,8,256]{3,2,1,0:T(8,128)S(1)} collective-permute-done((f32[10,1,8,256]{3,2,1,0:T(8,128)S(1)}, f32[10,1,8,256]{3,2,1,0:T(8,128)S(1)}, u32[]{:S(2)}, u32[]{:S(2)}) %collective-permute-start.8) | collective-permute-done | bytes 81952 | tf_op jit(solution)/shard_map/ppermute | solution.py:18
  97.3 2.9 %collective-permute-start.11 = (f32[10,10,1,256]{3,2,1,0:T(1,128)S(1)}, f32[10,10,1,256]{3,2,1,0:T(1,128)S(1)}, u32[]{:S(2)}, u32[]{:S(2)}) collective-permute-start(f32[10,10,1,256]{3,2,1,0:T(1,128)S(1)} %get-tuple-element.258), channel_id=1, source_target_pairs={{0,1},{1,2},{2,3},{3,4},{4,5},{5,6},{6,7},{7,8},{8,9},{9,10},{10,1... | collective-permute-start | bytes 307208 | tf_op jit(solution)/shard_map/ppermute | solution.py:17
  100.2 4.5 %collective-permute-start.10 = (f32[10,10,1,256]{3,2,1,0:T(1,128)S(1)}, f32[10,10,1,256]{3,2,1,0:T(1,128)S(1)}, u32[]{:S(2)}, u32[]{:S(2)}) collective-permute-start(f32[10,10,1,256]{3,2,1,0:T(1,128)S(1)} %get-tuple-element.257), channel_id=1, source_target_pairs={{1,0},{2,1},{3,2},{4,3},{5,4},{6,5},{7,6},{8,7},{9,8},{10,9},{11,1... | collective-permute-start | bytes 307208 | tf_op jit(solution)/shard_map/ppermute | solution.py:18
  106.7 2.1 %fusion.45 = f32[8,8,8,256]{3,2,1,0:T(8,128)S(1)} fusion(f32[8,8,8,256]{3,2,1,0:T(8,128)S(1)} %bitcast.75, f32[1,8,8,256]{3,2,1,0:T(8,128)S(1)} %collective-permute-done.6, f32[10,1,8,256]{3,2,1,0:T(8,128)S(1)} %collective-permute-done.9, f32[1,8,8,256]{3,2,1,0:T(8,128)S(1)} %collective-permute-done.7, f32[10,1,8,256]{3,2,1,0:T(8,128)S(1)} %collective-permute-done.8, ...), kind=kLoop, calls=%fused_computation.85 | loop fusion | flops 8781824 | bytes 1573888 | tf_op jit(solution)/shard_map/add | solution.py:105
  108.9 3.2 %collective-permute-start.12 = (f32[1,8,8,256]{3,2,1,0:T(8,128)S(1)}, f32[1,8,8,256]{3,2,1,0:T(8,128)S(1)}, u32[]{:S(2)}, u32[]{:S(2)}) collective-permute-start(f32[1,8,8,256]{3,2,1,0:T(8,128)S(1)} %get-tuple-element.264), channel_id=1, source_target_pairs={{64,0},{128,64},{192,128},{256,192},{320,256},{384,320},{448,384},... | collective-permute-start | bytes 196616 | tf_op jit(solution)/shard_map/ppermute | solution.py:18
  112.1 2.1 %collective-permute-start.13 = (f32[1,8,8,256]{3,2,1,0:T(8,128)S(1)}, f32[1,8,8,256]{3,2,1,0:T(8,128)S(1)}, u32[]{:S(2)}, u32[]{:S(2)}) collective-permute-start(f32[1,8,8,256]{3,2,1,0:T(8,128)S(1)} %get-tuple-element.263), channel_id=1, source_target_pairs={{0,64},{64,128},{128,192},{192,256},{256,320},{320,384},{384,448},... | collective-permute-start | bytes 196616 | tf_op jit(solution)/shard_map/ppermute | solution.py:17
  114.6 3.7 %collective-permute-done.13 = f32[1,8,8,256]{3,2,1,0:T(8,128)S(1)} collective-permute-done((f32[1,8,8,256]{3,2,1,0:T(8,128)S(1)}, f32[1,8,8,256]{3,2,1,0:T(8,128)S(1)}, u32[]{:S(2)}, u32[]{:S(2)}) %collective-permute-start.13) | collective-permute-done | bytes 65568 | tf_op jit(solution)/shard_map/ppermute | solution.py:17
  118.3 4.9 %collective-permute-start.15 = (f32[10,1,8,256]{3,2,1,0:T(8,128)S(1)}, f32[10,1,8,256]{3,2,1,0:T(8,128)S(1)}, u32[]{:S(2)}, u32[]{:S(2)}) collective-permute-start(f32[10,1,8,256]{3,2,1,0:T(8,128)S(1)} %get-tuple-element.260), channel_id=1, source_target_pairs={{0,16},{16,32},{32,48},{48,0},{1,17},{17,33},{33,49},{49,1},{2,18}... | collective-permute-start | bytes 245768 | tf_op jit(solution)/shard_map/ppermute | solution.py:17
  125.2 5.3 %collective-permute-done.14 = f32[10,1,8,256]{3,2,1,0:T(8,128)S(1)} collective-permute-done((f32[10,1,8,256]{3,2,1,0:T(8,128)S(1)}, f32[10,1,8,256]{3,2,1,0:T(8,128)S(1)}, u32[]{:S(2)}, u32[]{:S(2)}) %collective-permute-start.14) | collective-permute-done | bytes 81952 | tf_op jit(solution)/shard_map/ppermute | solution.py:18
  132.6 5.6 %collective-permute-start.16 = (f32[10,10,1,256]{3,2,1,0:T(1,128)S(1)}, f32[10,10,1,256]{3,2,1,0:T(1,128)S(1)}, u32[]{:S(2)}, u32[]{:S(2)}) collective-permute-start(f32[10,10,1,256]{3,2,1,0:T(1,128)S(1)} %get-tuple-element.255), channel_id=1, source_target_pairs={{1,0},{2,1},{3,2},{4,3},{5,4},{6,5},{7,6},{8,7},{9,8},{10,9},{11,1... | collective-permute-start | bytes 307208 | tf_op jit(solution)/shard_map/ppermute | solution.py:18
  139.8 2.9 %fusion.53 = f32[8,8,8,256]{3,2,1,0:T(8,128)} fusion(f32[8,8,8,256]{3,2,1,0:T(8,128)S(1)} %bitcast.76, f32[8,8,8,256]{3,2,1,0:T(8,128)S(1)} %fusion.45, f32[1,8,8,256]{3,2,1,0:T(8,128)S(1)} %collective-permute-done.12, f32[10,1,8,256]{3,2,1,0:T(8,128)S(1)} %collective-permute-done.15, f32[1,8,8,256]{3,2,1,0:T(8,128)S(1)} %collective-permute-done.13, ...), kind=kLoop, calls=%fused_computation.93 | loop fusion | flops 9043968 | bytes 2098176 | tf_op jit(solution)/shard_map/add | solution.py:108
  (94 shorter events, 34.9 us)
Async XLA Ops:
  0.0 33.5 %copy-start = (f32[8,8,8,256]{3,2,1,0:T(8,128)S(1)}, f32[8,8,8,256]{3,2,1,0:T(8,128)}, u32[]{:S(2)}) copy-start(f32[8,8,8,256]{3,2,1,0:T(8,128)} %param.16) | copy-start | bytes 1572868
  0.8 52.4 %collective-permute-start.1 = (f32[4,1,8,8]{3,2,1,0:T(8,128)S(1)}, f32[4,1,8,8]{3,2,1,0:T(8,128)S(1)}, u32[]{:S(2)}, u32[]{:S(2)}) collective-permute-start(f32[4,1,8,8]{3,2,1,0:T(8,128)S(1)} %get-tuple-element.276), channel_id=1, source_target_pairs={{64,0},{128,64},{192,128},{256,192},{320,256},{384,320},{448,384},... | collective-permute-start | bytes 3080 | tf_op jit(solution)/shard_map/ppermute | solution.py:18
  19.6 33.7 %collective-permute-start = (f32[4,1,8,8]{3,2,1,0:T(8,128)S(1)}, f32[4,1,8,8]{3,2,1,0:T(8,128)S(1)}, u32[]{:S(2)}, u32[]{:S(2)}) collective-permute-start(f32[4,1,8,8]{3,2,1,0:T(8,128)S(1)} %get-tuple-element.275), channel_id=1, source_target_pairs={{0,64},{64,128},{128,192},{192,256},{256,320},{320,384},{384,448},... | collective-permute-start | bytes 3080 | tf_op jit(solution)/shard_map/ppermute | solution.py:17
  33.5 1.6 %copy-start.4 = (s32[1024,256]{1,0:T(8,128)S(1)}, s32[1024,256]{1,0:T(8,128)}, u32[]{:S(2)}) copy-start(s32[1024,256]{1,0:T(8,128)} %param.18) | copy-start | bytes 3145732
  35.1 1.4 copy-start.3
  49.4 3.8 %copy-start.2 = (f32[3,8,8,8]{3,2,1,0:T(8,128)S(1)}, f32[3,8,8,8]{3,2,1,0:T(8,128)}, u32[]{:S(2)}) copy-start(f32[3,8,8,8]{3,2,1,0:T(8,128)} %param.21) | copy-start | bytes 18436
  49.5 3.8 %copy-start.5 = (f32[8,8,8]{2,1,0:T(8,128)S(1)}, f32[8,8,8]{2,1,0:T(8,128)}, u32[]{:S(2)}) copy-start(f32[8,8,8]{2,1,0:T(8,128)} %param.22) | copy-start | bytes 6148
  53.3 9.0 %collective-permute-start.3 = (f32[4,10,1,8]{3,2,1,0:T(1,128)S(1)}, f32[4,10,1,8]{3,2,1,0:T(1,128)S(1)}, u32[]{:S(2)}, u32[]{:S(2)}) collective-permute-start(f32[4,10,1,8]{3,2,1,0:T(1,128)S(1)} %get-tuple-element.274), channel_id=1, source_target_pairs={{16,0},{32,16},{48,32},{0,48},{17,1},{33,17},{49,33},{1,49},{18,2}... | collective-permute-start | bytes 3848 | tf_op jit(solution)/shard_map/ppermute | solution.py:18
  58.0 4.4 %collective-permute-start.2 = (f32[4,10,1,8]{3,2,1,0:T(1,128)S(1)}, f32[4,10,1,8]{3,2,1,0:T(1,128)S(1)}, u32[]{:S(2)}, u32[]{:S(2)}) collective-permute-start(f32[4,10,1,8]{3,2,1,0:T(1,128)S(1)} %get-tuple-element.273), channel_id=1, source_target_pairs={{0,16},{16,32},{32,48},{48,0},{1,17},{17,33},{33,49},{49,1},{2,18}... | collective-permute-start | bytes 3848 | tf_op jit(solution)/shard_map/ppermute | solution.py:17
  62.6 17.0 %collective-permute-start.5 = (f32[4,10,10,1]{3,2,1,0:T(8,128)S(1)}, f32[4,10,10,1]{3,2,1,0:T(8,128)S(1)}, u32[]{:S(2)}, u32[]{:S(2)}) collective-permute-start(f32[4,10,10,1]{3,2,1,0:T(8,128)S(1)} %get-tuple-element.272), channel_id=1, source_target_pairs={{1,0},{2,1},{3,2},{4,3},{5,4},{6,5},{7,6},{8,7},{9,8},{10,9},{11,1... | collective-permute-start | bytes 4808 | tf_op jit(solution)/shard_map/ppermute | solution.py:18
  71.9 13.2 %collective-permute-start.4 = (f32[4,10,10,1]{3,2,1,0:T(8,128)S(1)}, f32[4,10,10,1]{3,2,1,0:T(8,128)S(1)}, u32[]{:S(2)}, u32[]{:S(2)}) collective-permute-start(f32[4,10,10,1]{3,2,1,0:T(8,128)S(1)} %get-tuple-element.271), channel_id=1, source_target_pairs={{0,1},{1,2},{2,3},{3,4},{4,5},{5,6},{6,7},{7,8},{8,9},{9,10},{10,1... | collective-permute-start | bytes 4808 | tf_op jit(solution)/shard_map/ppermute | solution.py:17
  73.8 11.7 %collective-permute-start.6 = (f32[1,8,8,256]{3,2,1,0:T(8,128)S(1)}, f32[1,8,8,256]{3,2,1,0:T(8,128)S(1)}, u32[]{:S(2)}, u32[]{:S(2)}) collective-permute-start(f32[1,8,8,256]{3,2,1,0:T(8,128)S(1)} %get-tuple-element.266), channel_id=1, source_target_pairs={{64,0},{128,64},{192,128},{256,192},{320,256},{384,320},{448,384},... | collective-permute-start | bytes 196616 | tf_op jit(solution)/shard_map/ppermute | solution.py:18
  76.3 9.1 %collective-permute-start.7 = (f32[1,8,8,256]{3,2,1,0:T(8,128)S(1)}, f32[1,8,8,256]{3,2,1,0:T(8,128)S(1)}, u32[]{:S(2)}, u32[]{:S(2)}) collective-permute-start(f32[1,8,8,256]{3,2,1,0:T(8,128)S(1)} %get-tuple-element.265), channel_id=1, source_target_pairs={{0,64},{64,128},{128,192},{192,256},{256,320},{320,384},{384,448},... | collective-permute-start | bytes 196616 | tf_op jit(solution)/shard_map/ppermute | solution.py:17
  85.5 21.2 %copy-start.6 = (f32[256]{0:T(256)S(1)}, f32[256]{0:T(256)}, u32[]{:S(2)}) copy-start(f32[256]{0:T(256)} %param.23) | copy-start | bytes 3076
  85.5 6.4 %collective-permute-start.9 = (f32[10,1,8,256]{3,2,1,0:T(8,128)S(1)}, f32[10,1,8,256]{3,2,1,0:T(8,128)S(1)}, u32[]{:S(2)}, u32[]{:S(2)}) collective-permute-start(f32[10,1,8,256]{3,2,1,0:T(8,128)S(1)} %get-tuple-element.262), channel_id=1, source_target_pairs={{0,16},{16,32},{32,48},{48,0},{1,17},{17,33},{33,49},{49,1},{2,18}... | collective-permute-start | bytes 245768 | tf_op jit(solution)/shard_map/ppermute | solution.py:17
  89.9 7.3 %collective-permute-start.8 = (f32[10,1,8,256]{3,2,1,0:T(8,128)S(1)}, f32[10,1,8,256]{3,2,1,0:T(8,128)S(1)}, u32[]{:S(2)}, u32[]{:S(2)}) collective-permute-start(f32[10,1,8,256]{3,2,1,0:T(8,128)S(1)} %get-tuple-element.261), channel_id=1, source_target_pairs={{16,0},{32,16},{48,32},{0,48},{17,1},{33,17},{49,33},{1,49},{18,2}... | collective-permute-start | bytes 245768 | tf_op jit(solution)/shard_map/ppermute | solution.py:18
  97.3 7.7 %collective-permute-start.11 = (f32[10,10,1,256]{3,2,1,0:T(1,128)S(1)}, f32[10,10,1,256]{3,2,1,0:T(1,128)S(1)}, u32[]{:S(2)}, u32[]{:S(2)}) collective-permute-start(f32[10,10,1,256]{3,2,1,0:T(1,128)S(1)} %get-tuple-element.258), channel_id=1, source_target_pairs={{0,1},{1,2},{2,3},{3,4},{4,5},{5,6},{6,7},{7,8},{8,9},{9,10},{10,1... | collective-permute-start | bytes 307208 | tf_op jit(solution)/shard_map/ppermute | solution.py:17
  100.2 6.5 %collective-permute-start.10 = (f32[10,10,1,256]{3,2,1,0:T(1,128)S(1)}, f32[10,10,1,256]{3,2,1,0:T(1,128)S(1)}, u32[]{:S(2)}, u32[]{:S(2)}) collective-permute-start(f32[10,10,1,256]{3,2,1,0:T(1,128)S(1)} %get-tuple-element.257), channel_id=1, source_target_pairs={{1,0},{2,1},{3,2},{4,3},{5,4},{6,5},{7,6},{8,7},{9,8},{10,9},{11,1... | collective-permute-start | bytes 307208 | tf_op jit(solution)/shard_map/ppermute | solution.py:18
  108.9 5.8 %collective-permute-start.12 = (f32[1,8,8,256]{3,2,1,0:T(8,128)S(1)}, f32[1,8,8,256]{3,2,1,0:T(8,128)S(1)}, u32[]{:S(2)}, u32[]{:S(2)}) collective-permute-start(f32[1,8,8,256]{3,2,1,0:T(8,128)S(1)} %get-tuple-element.264), channel_id=1, source_target_pairs={{64,0},{128,64},{192,128},{256,192},{320,256},{384,320},{448,384},... | collective-permute-start | bytes 196616 | tf_op jit(solution)/shard_map/ppermute | solution.py:18
  112.1 6.2 %collective-permute-start.13 = (f32[1,8,8,256]{3,2,1,0:T(8,128)S(1)}, f32[1,8,8,256]{3,2,1,0:T(8,128)S(1)}, u32[]{:S(2)}, u32[]{:S(2)}) collective-permute-start(f32[1,8,8,256]{3,2,1,0:T(8,128)S(1)} %get-tuple-element.263), channel_id=1, source_target_pairs={{0,64},{64,128},{128,192},{192,256},{256,320},{320,384},{384,448},... | collective-permute-start | bytes 196616 | tf_op jit(solution)/shard_map/ppermute | solution.py:17
  118.3 6.8 %collective-permute-start.15 = (f32[10,1,8,256]{3,2,1,0:T(8,128)S(1)}, f32[10,1,8,256]{3,2,1,0:T(8,128)S(1)}, u32[]{:S(2)}, u32[]{:S(2)}) collective-permute-start(f32[10,1,8,256]{3,2,1,0:T(8,128)S(1)} %get-tuple-element.260), channel_id=1, source_target_pairs={{0,16},{16,32},{32,48},{48,0},{1,17},{17,33},{33,49},{49,1},{2,18}... | collective-permute-start | bytes 245768 | tf_op jit(solution)/shard_map/ppermute | solution.py:17
  123.2 7.3 %collective-permute-start.14 = (f32[10,1,8,256]{3,2,1,0:T(8,128)S(1)}, f32[10,1,8,256]{3,2,1,0:T(8,128)S(1)}, u32[]{:S(2)}, u32[]{:S(2)}) collective-permute-start(f32[10,1,8,256]{3,2,1,0:T(8,128)S(1)} %get-tuple-element.259), channel_id=1, source_target_pairs={{16,0},{32,16},{48,32},{0,48},{17,1},{33,17},{49,33},{1,49},{18,2}... | collective-permute-start | bytes 245768 | tf_op jit(solution)/shard_map/ppermute | solution.py:18
  130.6 7.7 %collective-permute-start.17 = (f32[10,10,1,256]{3,2,1,0:T(1,128)S(1)}, f32[10,10,1,256]{3,2,1,0:T(1,128)S(1)}, u32[]{:S(2)}, u32[]{:S(2)}) collective-permute-start(f32[10,10,1,256]{3,2,1,0:T(1,128)S(1)} %get-tuple-element.256), channel_id=1, source_target_pairs={{0,1},{1,2},{2,3},{3,4},{4,5},{5,6},{6,7},{7,8},{8,9},{9,10},{10,1... | collective-permute-start | bytes 307208 | tf_op jit(solution)/shard_map/ppermute | solution.py:17
  132.6 7.3 %collective-permute-start.16 = (f32[10,10,1,256]{3,2,1,0:T(1,128)S(1)}, f32[10,10,1,256]{3,2,1,0:T(1,128)S(1)}, u32[]{:S(2)}, u32[]{:S(2)}) collective-permute-start(f32[10,10,1,256]{3,2,1,0:T(1,128)S(1)} %get-tuple-element.255), channel_id=1, source_target_pairs={{1,0},{2,1},{3,2},{4,3},{5,4},{6,5},{7,6},{8,7},{9,8},{10,9},{11,1... | collective-permute-start | bytes 307208 | tf_op jit(solution)/shard_map/ppermute | solution.py:18
  (1 other events, 1.3 us)
where the time goes:
time: 145 us; the launch traced here: 143 us
  starting transfers between devices  78.4 us (54%)
  waiting for transfers between devices  23.7 us (16%)
  other arithmetic  19.9 us (14%)
  matrix products  9.14 us (6%)
  local copies, waits for them, and re-layouts  8.26 us (6%)
  between operations  3.04 us (2%)
    ppermute x9, starting transfers between devices, with_halo(): after = lax.ppermute(initial, axis, down)  52.3 us
    ppermute x9, starting transfers between devices, with_halo(): before = lax.ppermute(last, axis, up)  26 us
    ppermute x9, waiting for transfers between devices, with_halo(): after = lax.ppermute(initial, axis, down)  14.3 us
    ppermute x9, waiting for transfers between devices, with_halo(): before = lax.ppermute(last, axis, up)  9.42 us
    dot_general x6, matrix products, react(): lax.dot_general(logs, reactant_table, (((1,), (1,)), ((), ())), precision...  7.31 us
    sort x1, other arithmetic, integrate(): order = jnp.argsort(-counts)  3.77 us
    sort x1, other arithmetic, integrate(): inverse = jnp.argsort(order)  3.77 us
    gather x1, local copies, waits for them, and re-layouts, integrate(): sorted_counts = counts[order]  3.49 us
  transfers between devices with their start and end apart: 18, of which 9 were waited for; matrix products, arithmetic and copies ran while one was open for 21% of the time, Pallas kernels for 0%

commit v1 on v0

v1 whole, which is shorter than its diff:
```python
import functools

import jax
import jax.numpy as jnp
from jax import lax
from jax.experimental import pallas as pl
from jax.experimental.pallas import tpu as pltpu
from jax.sharding import PartitionSpec as P

MESH = pl.DeviceIdType.MESH
MAX_SUB = 4
F32 = jnp.float32
BF16 = jnp.bfloat16
DIRS = (("gx", 1), ("gx", -1), ("gy", 1), ("gy", -1), ("gz", 1), ("gz", -1))


def lane_column(row, mask):
    picked = jnp.where(mask, jnp.broadcast_to(row, mask.shape), 0.0)
    return jnp.broadcast_to(jnp.sum(picked, axis=1, keepdims=True), (8, 128))


def twice(c):
    return jnp.concatenate([c, c], axis=1)


def kernel(
    sizes,
    species,
    reactants,
    products,
    counts,
    rate,
    velocity,
    viscosity,
    diffusivity,
    out,
    react_i,
    prod_i,
    table,
    stoich,
    v1,
    v2,
    pack1,
    pack2,
    z1,
    z2,
    result,
    hx,
    hy,
    hz,
    nu,
    hzm,
    nzlo,
    nzhi,
    csend,
    crecv,
    load_sem,
    out_sem,
    send_sem,
    recv_sem,
):
    def toward(k):
        axis, step = DIRS[k]
        n = sizes[axis]
        return {axis: lax.rem(lax.axis_index(axis) + (step + n), n)}

    barrier = pltpu.get_barrier_semaphore()
    for k in range(6):
        pl.semaphore_signal(barrier, inc=1, device_id=toward(k), device_id_type=MESH)

    loads = [
        pltpu.make_async_copy(reactants, react_i, load_sem.at[0]),
        pltpu.make_async_copy(species.at[pl.ds(6, 2)], v1.at[pl.ds(7, 2), pl.ds(1, 8)], load_sem.at[1]),
        pltpu.make_async_copy(products, prod_i, load_sem.at[2]),
        pltpu.make_async_copy(species.at[pl.ds(0, 6)], v1.at[pl.ds(1, 6), pl.ds(1, 8)], load_sem.at[3]),
    ]
    for copy in loads:
        copy.start()

    sub = lax.broadcasted_iota(jnp.int32, (8, 8), 0)
    lane = lax.broadcasted_iota(jnp.int32, (8, 8), 1)
    eye = sub == lane

    def expand(x, _):
        for y in range(8):
            hx[1 + x, y] = 0.5 * lane_column(velocity[0, x, y : y + 1, :], eye)
            hy[x, 1 + y] = 0.5 * lane_column(velocity[1, x, y : y + 1, :], eye)
            hz[x, y] = 0.5 * lane_column(velocity[2, x, y : y + 1, :], eye)
            nu[1 + x, 1 + y] = 0.5 * lane_column(viscosity[x, y : y + 1, :], eye)
        for k, row in ((2, 7), (3, 0)):
            csend[k, 0, pl.ds(x, 1), 0:8] = velocity[1, x, row : row + 1, :]
            csend[k, 1, pl.ds(x, 1), 0:8] = viscosity[x, row : row + 1, :]
        for k, col in ((4, 7), (5, 0)):
            for slot, tile in ((0, velocity[2, x]), (1, viscosity[x])):
                column = jnp.sum(jnp.where(lane == col, tile, 0.0), axis=1, keepdims=True)
                row = jnp.sum(jnp.where(eye, jnp.broadcast_to(column, (8, 8)), 0.0), axis=0, keepdims=True)
                csend[k, slot, pl.ds(x, 1), 0:8] = row
        return 0

    lax.fori_loop(0, 8, expand, 0)
    for k, plane in ((0, 7), (1, 0)):
        csend[k, 0, :, 0:8] = velocity[0, plane]
        csend[k, 1, :, 0:8] = viscosity[plane]

    loads[0].wait()
    rb = react_i[...].astype(F32).astype(BF16)
    table[:, 0:256] = rb
    table[:, 256:512] = rb
    stoich[:, 256:512] = rb
    loads[2].wait()
    stoich[:, 0:256] = prod_i[...].astype(F32).astype(BF16)

    def chemistry(first_block, blocks):
        rows = blocks * 128
        planes = pl.ds(1 + 2 * first_block, 2 * blocks)

        def level_step(level, _):
            conc = v1[planes, 1:9].reshape(rows, 256)
            logs = jnp.log(conc)
            high = logs.astype(BF16)
            low = (logs - high.astype(F32)).astype(BF16)
            both = jnp.concatenate([high, low], axis=1)
            expo = lax.dot_general(both, table[...], (((1,), (1,)), ((), ())), preferred_element_type=F32)
            rates = (rate[...] * jnp.exp(expo)).astype(BF16)
            terms = jnp.dot(rates, stoich[...], preferred_element_type=F32)
            for b in range(blocks):
                count = jnp.full((1, 256), counts[first_block + b], jnp.int32)
                length = 1.0 / count.astype(F32)
                part = slice(128 * b, 128 * b + 128)
                old = conc[part]
                fresh = old * (old + length * terms[part, 0:256]) / (old + length * terms[part, 256:512])
                new = jnp.where(count >= level, fresh, old)
                v1[pl.ds(1 + 2 * (first_block + b), 2), 1:9] = new.reshape(2, 8, 8, 256)
            return 0

        lax.fori_loop(1, MAX_SUB + 1, level_step, 0)

    def pack(field, packed, x):
        for y in range(8):
            packed[0, x, y : y + 1, :] = field[1 + x, 1 + y, 0:1, :]
            packed[1, x, y : y + 1, :] = field[1 + x, 1 + y, 7:8, :]

    used = []

    def message(k, src, dst):
        i = len(used)
        copy = pltpu.make_async_remote_copy(
            src_ref=src,
            dst_ref=dst,
            send_sem=send_sem.at[i],
            recv_sem=recv_sem.at[i],
            device_id=toward(k),
            device_id_type=MESH,
        )
        used.append(copy)
        copy.start()
        return copy

    def send_x(k, field):
        src, dst = (8, 0) if k == 0 else (1, 9)
        return message(k, field.at[src, pl.ds(1, 8)], field.at[dst, pl.ds(1, 8)])

    def send_yz(field, packed, halo, x0, n):
        xs, ps = pl.ds(1 + x0, n), pl.ds(x0, n)
        return [
            message(2, field.at[xs, 8], field.at[xs, 0]),
            message(3, field.at[xs, 1], field.at[xs, 9]),
            message(4, packed.at[1, ps], halo.at[0, ps]),
            message(5, packed.at[0, ps], halo.at[1, ps]),
        ]

    row8 = lax.broadcasted_iota(jnp.int32, (8, 128), 0)
    row8w = lax.broadcasted_iota(jnp.int32, (8, 256), 0)
    diff = diffusivity[...]

    def operate(field, halo, x, y):
        v = field[1 + x, 1 + y]
        n = nu[1 + x, 1 + y]
        h = hz[x, y]
        up = jnp.where(row8w == 7, halo[1, x, y : y + 1, :], pltpu.roll(v, 7, 0))
        down = jnp.where(row8w == 0, halo[0, x, y : y + 1, :], pltpu.roll(v, 1, 0))
        h_down = jnp.where(row8 == 0, hzm[x, y : y + 1, :], pltpu.roll(h, 1, 0))
        n_up = jnp.where(row8 == 7, nzhi[x, y : y + 1, :], pltpu.roll(n, 7, 0))
        n_down = jnp.where(row8 == 0, nzlo[x, y : y + 1, :], pltpu.roll(n, 1, 0))
        carried, spread = None, None
        for ahead, behind, h0, h1, n0, n1 in (
            (field[2 + x, 1 + y], field[x, 1 + y], hx[1 + x, y], hx[x, y], nu[2 + x, 1 + y], nu[x, 1 + y]),
            (field[1 + x, 2 + y], field[1 + x, y], hy[x, 1 + y], hy[x, y], nu[1 + x, 2 + y], nu[1 + x, y]),
            (up, down, h, h_down, n_up, n_down),
        ):
            flow = twice(h0) * (v + ahead) - twice(h1) * (behind + v)
            mix = twice(n + n0) * (ahead - v) - twice(n1 + n) * (v - behind)
            carried = flow if carried is None else carried + flow
            spread = mix if spread is None else spread + mix
        return v, diff * spread - carried

    def advance(x):
        for y in range(8):
            v, change = operate(v1, z1, x, y)
            v2[1 + x, 1 + y] = v + change
        pack(v2, pack2, x)

    def finish(x):
        for y in range(8):
            v, change = operate(v2, z2, x, y)
            result[x, y] = 0.5 * v1[1 + x, 1 + y] + 0.5 * (v + change)

    def each(lo, hi, body):
        def step(x, _):
            body(x)
            return 0

        lax.fori_loop(lo, hi, step, 0)

    loads[1].wait()
    chemistry(3, 1)
    each(6, 8, lambda x: pack(v1, pack1, x))
    pl.semaphore_wait(barrier, 6)
    coefs = [message(k, csend.at[k], crecv.at[k]) for k in range(6)]
    r_xup = send_x(0, v1)
    r_last = send_yz(v1, pack1, z1, 6, 2)

    loads[3].wait()
    chemistry(0, 3)
    each(0, 6, lambda x: pack(v1, pack1, x))
    r_xdown = send_x(1, v1)
    r_rest = send_yz(v1, pack1, z1, 0, 6)

    for k in (1, 2, 3, 4, 5):
        coefs[k].wait_recv()
    for i in range(8):
        hy[i, 0] = 0.5 * lane_column(crecv[2, 0, i : i + 1, 0:8], eye)
        nu[1 + i, 0] = 0.5 * lane_column(crecv[2, 1, i : i + 1, 0:8], eye)
        nu[1 + i, 9] = 0.5 * lane_column(crecv[3, 1, i : i + 1, 0:8], eye)
        nu[9, 1 + i] = 0.5 * lane_column(crecv[1, 1, i : i + 1, 0:8], eye)
        hzm[i] = 0.5 * lane_column(crecv[4, 0, i : i + 1, 0:8], eye)
        nzlo[i] = 0.5 * lane_column(crecv[4, 1, i : i + 1, 0:8], eye)
        nzhi[i] = 0.5 * lane_column(crecv[5, 1, i : i + 1, 0:8], eye)

    for copy in r_last:
        copy.wait_recv()
    r_xdown.wait_recv()
    advance(7)
    f_xup = send_x(0, v2)
    for copy in r_rest:
        copy.wait_recv()
    each(1, 7, advance)
    f_rest = send_yz(v2, pack2, z2, 1, 7)
    coefs[0].wait_recv()
    for i in range(8):
        hx[0, i] = 0.5 * lane_column(crecv[0, 0, i : i + 1, 0:8], eye)
        nu[0, 1 + i] = 0.5 * lane_column(crecv[0, 1, i : i + 1, 0:8], eye)
    r_xup.wait_recv()
    advance(0)
    f_first = send_yz(v2, pack2, z2, 0, 1)
    f_xdown = send_x(1, v2)

    for copy in f_rest:
        copy.wait_recv()
    each(1, 7, finish)
    middle = pltpu.make_async_copy(result.at[pl.ds(1, 6)], out.at[pl.ds(1, 6)], out_sem.at[0])
    middle.start()
    f_xdown.wait_recv()
    finish(7)
    final = pltpu.make_async_copy(result.at[7], out.at[7], out_sem.at[1])
    final.start()
    for copy in f_first:
        copy.wait_recv()
    f_xup.wait_recv()
    finish(0)
    initial = pltpu.make_async_copy(result.at[0], out.at[0], out_sem.at[2])
    initial.start()
    for copy in used:
        copy.wait_send()
    middle.wait()
    final.wait()
    initial.wait()


def shards(sizes, species, substeps, reactants, products, rate_const, velocity, viscosity, diffusivity):
    any_space = pl.BlockSpec(memory_space=pl.ANY)
    vmem = pl.BlockSpec(memory_space=pltpu.VMEM)
    messages = 26
    return pl.pallas_call(
        functools.partial(kernel, sizes),
        out_shape=jax.ShapeDtypeStruct(species.shape, F32),
        in_specs=[any_space] * 3 + [pl.BlockSpec(memory_space=pltpu.SMEM)] + [vmem] * 4,
        out_specs=any_space,
        scratch_shapes=[
            pltpu.VMEM((1024, 256), jnp.int32),
            pltpu.VMEM((1024, 256), jnp.int32),
            pltpu.VMEM((1024, 512), BF16),
            pltpu.VMEM((1024, 512), BF16),
            pltpu.VMEM((10, 10, 8, 256), F32),
            pltpu.VMEM((10, 10, 8, 256), F32),
            pltpu.VMEM((2, 8, 8, 256), F32),
            pltpu.VMEM((2, 8, 8, 256), F32),
            pltpu.VMEM((2, 8, 8, 256), F32),
            pltpu.VMEM((2, 8, 8, 256), F32),
            pltpu.VMEM((8, 8, 8, 256), F32),
            pltpu.VMEM((9, 8, 8, 128), F32),
            pltpu.VMEM((8, 9, 8, 128), F32),
            pltpu.VMEM((8, 8, 8, 128), F32),
            pltpu.VMEM((10, 10, 8, 128), F32),
            pltpu.VMEM((8, 8, 128), F32),
            pltpu.VMEM((8, 8, 128), F32),
            pltpu.VMEM((8, 8, 128), F32),
            pltpu.VMEM((6, 2, 8, 128), F32),
            pltpu.VMEM((6, 2, 8, 128), F32),
            pltpu.SemaphoreType.DMA((4,)),
            pltpu.SemaphoreType.DMA((3,)),
            pltpu.SemaphoreType.DMA((messages,)),
            pltpu.SemaphoreType.DMA((messages,)),
        ],
        compiler_params=pltpu.CompilerParams(
            collective_id=0, has_side_effects=True, vmem_limit_bytes=63 * 2**20
        ),
    )(
        species,
        reactants,
        products,
        substeps.reshape(-1),
        rate_const.reshape(1, -1),
        velocity,
        viscosity,
        diffusivity.reshape(1, -1),
    )


def solution(mesh):
    return jax.shard_map(
        functools.partial(shards, dict(mesh.shape)),
        mesh=mesh,
        in_specs=(
            P("gx", "gy", "gz", None),
            P("gx", "gy", "gz"),
            P(),
            P(),
            P(),
            P(None, "gx", "gy", "gz"),
            P("gx", "gy", "gz"),
            P(),
        ),
        out_specs=P("gx", "gy", "gz", None),
        check_vma=False,
    )
```

time: 145 us -> 39.9 us (0.28); the launches traced: 143 us -> 39.7 us
  starting transfers between devices: 78.4 us -> 0 us
  Pallas kernels: 0 us -> 37.8 us
  waiting for transfers between devices: 23.7 us -> 0 us
  other arithmetic: 19.9 us -> 0 us
  matrix products: 9.14 us -> 0 us
  local copies, waits for them, and re-layouts: 8.26 us -> 1.87 us
  between operations: 3.04 us -> 0.01 us
    ppermute x18 -> x0, starting transfers between devices: 78.4 us -> none  [the longest x9 52.3 us: with_halo(): after = lax.ppermute(initial, axis, down)]
    pallas_call x0 -> x1, Pallas kernels: none -> 37.8 us  [shards(): pl.pallas_call(functools.partial(kernel, sizes), out_shape=jax.ShapeDtype...]
    ppermute x18 -> x0, waiting for transfers between devices: 23.7 us -> none  [the longest x9 14.3 us: with_halo(): after = lax.ppermute(initial, axis, down)]
    dot_general x12 -> x0, matrix products: 9.14 us -> none  [the longest x6 7.31 us: react(): lax.dot_general(logs, reactant_table, (((1,), (1,)), ((), ())), precision...]
    sort x2 -> x0, other arithmetic: 7.54 us -> none  [the longest x1 3.77 us: integrate(): order = jnp.argsort(-counts)]
    gather x3 -> x0, local copies, waits for them, and re-layouts: 6.64 us -> none  [the longest x1 3.49 us: integrate(): sorted_counts = counts[order]]
    add x2 -> x0, other arithmetic: 5.04 us -> none  [the longest x1 2.9 us: shards(): return 0.5 * field + 0.5 * second]
    another operation x2 -> x0, other arithmetic: 1.77 us -> none
  transfers between devices with their start and end apart: 18 -> 0, of which waited for: 9 -> 0; matrix products, arithmetic and copies ran while one was open for 21% -> 0% of each run, Pallas kernels for 0% -> 0%
where the time goes in v1:
time: 39.9 us; the launch traced here: 39.7 us
  Pallas kernels  37.8 us (95%)
  local copies, waits for them, and re-layouts  1.87 us (5%)
    pallas_call x1, Pallas kernels, shards(): pl.pallas_call(functools.partial(kernel, sizes), out_shape=jax.ShapeDtype...  37.8 us
    unnamed x1, local copies, waits for them, and re-layouts  1.87 us

profile of v1, /device:TPU:1, one launch (start us, length us, event | category | flops | bytes accessed | tf_op | source)
XLA Modules:
  0.0 39.7 jit_solution(8377759091882067153)
XLA Ops:
  0.0 37.8 %shard_map.82 = f32[8,8,8,256]{3,2,1,0:T(8,128)} custom-call(f32[8,8,8,256]{3,2,1,0:T(8,128)} %species.1, s32[1024,256]{1,0:T(8,128)} %reactants.1, s32[1024,256]{1,0:T(8,128)} %products.1, s32[4]{0:T(128)} %bitcast.5, f32[1,1024]{1,0:T(1,128)} %bitcast.3, f32[3,8,8,8]{3,2,1,0:T(8,128)} %velocity.1, f32[8,8,8]{2,1,0:T(8,128)} %viscosity.1, f32[1,256]{1,0:T(1,128)} %bitcast.4), custom_call_target="tpu_custom_call" | custom-call | tf_op jit(solution)/shard_map/pallas_call | solution.py:284
  37.8 1.9 %copy.10 = f32[8,8,8,256]{3,2,1,0:T(8,128)} copy(f32[8,8,8,256]{3,2,1,0:T(8,128)} %shard_map.82) | data formatting | bytes 1048576

commit v2 on v0

v2 whole, which is shorter than its diff:
```python
import functools

import jax
import jax.numpy as jnp
from jax import lax
from jax.experimental import pallas as pl
from jax.experimental.pallas import tpu as pltpu
from jax.sharding import PartitionSpec as P

MESH = pl.DeviceIdType.MESH
MAX_SUB = 4
F32 = jnp.float32
BF16 = jnp.bfloat16
AXES = ("gx", "gy", "gz")
FACES = ((1, 0, 0), (-1, 0, 0), (0, 1, 0), (0, -1, 0), (0, 0, 1), (0, 0, -1))
EDGES = tuple((a, b, 0) for a in (1, -1) for b in (1, -1))
EDGES += tuple((a, 0, c) for a in (1, -1) for c in (1, -1))
EDGES += tuple((0, b, c) for b in (1, -1) for c in (1, -1))
AHEAD = tuple(s for s in FACES + EDGES if s[0] == 1)
GREETED = tuple(s for s in FACES + EDGES if s[0] != 1)


def twice(c):
    return jnp.concatenate([c, c], axis=1)


def kernel(
    sizes,
    species,
    reactants,
    products,
    substeps,
    rate_const,
    velocity,
    viscosity,
    diffusivity,
    out,
    react_i,
    prod_i,
    counts,
    rate,
    coef,
    diff_ref,
    table,
    stoich,
    v1,
    v2,
    zp,
    zf,
    yzp,
    yz,
    z2,
    k1,
    kzp,
    kx,
    ky,
    kz,
    kyz,
    kx_in,
    ky_in,
    kz_in,
    ke_in,
    kyz_in,
    spread,
    zspread,
    yzspread,
    result,
    load_sem,
    out_sem,
    send_sem,
    recv_sem,
    entry_sem,
):
    def toward(steps):
        place = {}
        for axis, step in zip(AXES, steps):
            if step:
                n = sizes[axis]
                place[axis] = lax.rem(lax.axis_index(axis) + (step + n), n)
        return place

    barrier = pltpu.get_barrier_semaphore()
    for steps in GREETED:
        pl.semaphore_signal(barrier, inc=1, device_id=toward(steps), device_id_type=MESH)

    loads = []
    for src, dst in (
        (reactants, react_i),
        (species.at[pl.ds(6, 2)], v1.at[pl.ds(8, 2), pl.ds(2, 8)]),
        (rate_const, rate),
        (substeps, counts),
        (products, prod_i),
        (species.at[pl.ds(0, 6)], v1.at[pl.ds(2, 6), pl.ds(2, 8)]),
        (velocity, coef.at[pl.ds(0, 3)]),
        (viscosity, coef.at[3]),
        (diffusivity, diff_ref),
    ):
        copy = pltpu.make_async_copy(src, dst, load_sem.at[len(loads)])
        copy.start()
        loads.append(copy)

    eye = lax.broadcasted_iota(jnp.int32, (8, 8), 0) == lax.broadcasted_iota(jnp.int32, (8, 8), 1)
    row = lax.broadcasted_iota(jnp.int32, (8, 128), 0)
    row_wide = lax.broadcasted_iota(jnp.int32, (8, 256), 0)
    lane = lax.broadcasted_iota(jnp.int32, (8, 128), 1)
    kind, place = lax.rem(lane, 4), lane // 4

    def each(lo, hi, body):
        def step(x, _):
            body(x)
            return 0

        lax.fori_loop(lo, hi, step, 0)

    def pack_z(field, base, packed, x):
        for layer, z in enumerate((0, 1, 6, 7)):
            for y in range(8):
                packed[layer, x, y : y + 1, :] = field[base + x, base + y, z : z + 1, :]

    def pack_yz(field, base, packed):
        for i, (y, z) in enumerate(((7, 7), (7, 0), (0, 7), (0, 0))):
            for x in range(8):
                packed[i, x : x + 1, :] = field[base + x, base + y, z : z + 1, :]

    used = []

    def message(steps, src, dst):
        i = len(used)
        copy = pltpu.make_async_remote_copy(
            src_ref=src,
            dst_ref=dst,
            send_sem=send_sem.at[i],
            recv_sem=recv_sem.at[i],
            device_id=toward(steps),
            device_id_type=MESH,
        )
        used.append(copy)
        return copy

    def start(copies):
        for copy in copies:
            copy.start()
        return copies

    own = pl.ds(2, 8)

    def send_plus(field, packed, halo):
        n = 2
        copies = [message((1, 0, 0), field.at[pl.ds(8, n), own], field.at[pl.ds(0, n), own])]
        copies.append(message((1, 1, 0), field.at[9, 9], field.at[1, 1]))
        copies.append(message((1, -1, 0), field.at[9, 2], field.at[1, 10]))
        copies.append(message((1, 0, 1), packed.at[3, 7], halo.at[1, 0]))
        copies.append(message((1, 0, -1), packed.at[0, 7], halo.at[2, 0]))
        return copies

    def send_minus(field, packed, halo):
        copies = [message((-1, 0, 0), field.at[pl.ds(2, 2), own], field.at[pl.ds(10, 2), own])]
        copies.append(message((-1, 1, 0), field.at[2, 9], field.at[10, 1]))
        copies.append(message((-1, -1, 0), field.at[2, 2], field.at[10, 10]))
        copies.append(message((-1, 0, 1), packed.at[3, 0], halo.at[1, 9]))
        copies.append(message((-1, 0, -1), packed.at[0, 0], halo.at[2, 9]))
        return copies

    def send_side(field, packed, halo, edges, edge_halo):
        mid = pl.ds(1, 8)
        lo, hi = pl.ds(0, 2), pl.ds(2, 2)
        copies = [
            message((0, 1, 0), field.at[own, pl.ds(8, 2)], field.at[own, pl.ds(0, 2)]),
            message((0, -1, 0), field.at[own, pl.ds(2, 2)], field.at[own, pl.ds(10, 2)]),
            message((0, 0, 1), packed.at[hi], halo.at[lo, mid]),
            message((0, 0, -1), packed.at[lo], halo.at[hi, mid]),
        ]
        for i, steps in enumerate(EDGES[8:]):
            copies.append(message(steps, edges.at[i], edge_halo.at[i]))
        return copies

    def widen(tile, place):
        at = 4 * place
        return [jnp.broadcast_to(tile[:, at + c : at + c + 1], (8, 128)) for c in range(4)]

    def own_coefficients(x):
        rows_x = None
        for y in range(8):
            merged = None
            for c in range(4):
                line = coef[c, x, y : y + 1, :]
                picked = jnp.where(eye, jnp.broadcast_to(line, (8, 8)), 0.0)
                column = jnp.broadcast_to(0.5 * jnp.sum(picked, axis=1, keepdims=True), (8, 128))
                spread[2 + x, 2 + y, c] = column
                merged = column if c == 0 else jnp.where(kind == c, column, merged)
            k1[x, y] = merged
            rows_x = merged if y == 0 else jnp.where(place == y, merged, rows_x)
            ky[y] = jnp.where(place == x, merged, ky[y])
        kx[x] = rows_x
        pack_z(k1, 0, kzp, x)
        for layer in range(4):
            kz[layer] = jnp.where(place == x, kzp[layer, x], kz[layer])
        for layer, clayer in ((0, 2), (3, 3)):
            for c, value in enumerate(widen(kzp[layer, x], 0)):
                zspread[clayer, 1 + x, c] = value

    def send_coefficients():
        pack_yz(k1, 0, kyz)
        lo, hi = pl.ds(0, 2), pl.ds(6, 2)
        plus = [message((1, 0, 0), kx.at[hi], kx_in.at[0])]
        plus.append(message((1, 1, 0), kx.at[7], ke_in.at[0]))
        plus.append(message((1, -1, 0), kx.at[7], ke_in.at[1]))
        plus.append(message((1, 0, 1), kz.at[3], ke_in.at[4]))
        plus.append(message((1, 0, -1), kz.at[0], ke_in.at[5]))
        minus = [message((-1, 0, 0), kx.at[lo], kx_in.at[1])]
        minus.append(message((-1, 1, 0), kx.at[0], ke_in.at[2]))
        minus.append(message((-1, -1, 0), kx.at[0], ke_in.at[3]))
        minus.append(message((-1, 0, 1), kz.at[3], ke_in.at[6]))
        minus.append(message((-1, 0, -1), kz.at[0], ke_in.at[7]))
        side = [message((0, 1, 0), ky.at[hi], ky_in.at[0])]
        side.append(message((0, -1, 0), ky.at[lo], ky_in.at[1]))
        side.append(message((0, 0, 1), kz.at[pl.ds(2, 2)], kz_in.at[0]))
        side.append(message((0, 0, -1), kz.at[lo], kz_in.at[1]))
        for i, steps in enumerate(EDGES[8:]):
            side.append(message(steps, kyz.at[i], kyz_in.at[i]))
        return start(plus), minus, start(side)

    loads[0].wait()
    rb = react_i[...].astype(F32).astype(BF16)
    table[:, 0:256] = rb
    table[:, 256:512] = rb
    stoich[:, 256:512] = rb
    for i in (1, 2, 3, 4):
        loads[i].wait()
    stoich[:, 0:256] = prod_i[...].astype(F32).astype(BF16)

    def chemistry(first_block, blocks, from_level, to_level, beside=None):
        rows = blocks * 128
        planes = pl.ds(2 + 2 * first_block, 2 * blocks)

        def level_step(level, _):
            conc = v1[planes, 2:10].reshape(rows, 256)
            logs = jnp.log(conc)
            high = logs.astype(BF16)
            low = (logs - high.astype(F32)).astype(BF16)
            both = jnp.concatenate([high, low], axis=1)
            if beside is not None:
                beside(level)
            expo = lax.dot_general(both, table[...], (((1,), (1,)), ((), ())), preferred_element_type=F32)
            rates = (rate[...] * jnp.exp(expo)).astype(BF16)
            terms = jnp.dot(rates, stoich[...], preferred_element_type=F32)
            for b in range(blocks):
                count = jnp.full((1, 256), counts[first_block + b], jnp.int32)
                length = 1.0 / count.astype(F32)
                part = slice(128 * b, 128 * b + 128)
                old = conc[part]
                fresh = old * (old + length * terms[part, 0:256]) / (old + length * terms[part, 256:512])
                new = jnp.where(count >= level, fresh, old)
                v1[pl.ds(2 + 2 * (first_block + b), 2), 2:10] = new.reshape(2, 8, 8, 256)
            return 0

        lax.fori_loop(from_level, to_level + 1, level_step, 0)

    def flux(diff, v, n, parts):
        carried, mixed = None, None
        for ahead, behind, h0, h1, n0, n1 in parts:
            flow = twice(h0) * (v + ahead) - twice(h1) * (behind + v)
            mix = twice(n + n0) * (ahead - v) - twice(n1 + n) * (v - behind)
            carried = flow if carried is None else carried + flow
            mixed = mix if mixed is None else mixed + mix
        return diff * mixed - carried

    def shift(value, rows, below, above):
        up = jnp.where(rows == 7, above, pltpu.roll(value, 7, 0))
        down = jnp.where(rows == 0, below, pltpu.roll(value, 1, 0))
        return up, down

    def column(field, base, x, y, below, above, coef_below, coef_above):
        fx, fy, cx, cy = x + base, y + base, x + 2, y + 2
        v, n, h = field[fx, fy], spread[cx, cy, 3], spread[cx, cy, 2]
        up, down = shift(v, row_wide, below, above)
        n_up, n_down = shift(n, row, coef_below(3), coef_above(3))
        h_down = jnp.where(row == 0, coef_below(2), pltpu.roll(h, 1, 0))
        parts = (
            (field[fx + 1, fy], field[fx - 1, fy], spread[cx, cy, 0], spread[cx - 1, cy, 0], spread[cx + 1, cy, 3], spread[cx - 1, cy, 3]),
            (field[fx, fy + 1], field[fx, fy - 1], spread[cx, cy, 1], spread[cx, cy - 1, 1], spread[cx, cy + 1, 3], spread[cx, cy - 1, 3]),
            (up, down, h, h_down, n_up, n_down),
        )
        return v, flux(diff_ref[...], v, n, parts)

    def zcoef(layer, x, y):
        return lambda c: zspread[layer, 1 + x, c, y : y + 1, :]

    def yzcoef(i, x):
        return lambda c: yzspread[i, c, pl.ds(x, 1), :]

    def first_plane(x):
        for y in range(8):
            below, above = zf[1, 1 + x, y : y + 1, :], zf[2, 1 + x, y : y + 1, :]
            v, change = column(v1, 2, x, y, below, above, zcoef(1, x, y), zcoef(4, x, y))
            v2[1 + x, 1 + y] = v + change

    def first_rim(x):
        for y, i, j in ((-1, 0, 1), (8, 2, 3)):
            below, above = yz[i, pl.ds(x, 1), :], yz[j, pl.ds(x, 1), :]
            v, change = column(v1, 2, x, y, below, above, yzcoef(i, x), yzcoef(j, x))
            v2[1 + x, 1 + y] = v + change
        for side, layer, clayer, i, j in ((0, 1, 1, 0, 2), (1, 2, 4, 1, 3)):
            v, n, h = zf[layer, 1 + x], zspread[clayer, 1 + x, 3], zspread[clayer, 1 + x, 1]
            up, down = shift(v, row_wide, yz[i, pl.ds(x, 1), :], yz[j, pl.ds(x, 1), :])
            n_up, n_down = shift(n, row, yzcoef(i, x)(3), yzcoef(j, x)(3))
            h_down = jnp.where(row == 0, yzcoef(i, x)(1), pltpu.roll(h, 1, 0))
            ahead = zp[0, x] if side == 0 else zf[3, 1 + x]
            behind = zf[0, 1 + x] if side == 0 else zp[3, x]
            c = 1 + x
            parts = (
                (zf[layer, c + 1], zf[layer, c - 1], zspread[clayer, c, 0], zspread[clayer, c - 1, 0], zspread[clayer, c + 1, 3], zspread[clayer, c - 1, 3]),
                (up, down, h, h_down, n_up, n_down),
                (ahead, behind, zspread[clayer, c, 2], zspread[clayer - 1, c, 2], zspread[clayer + 1, c, 3], zspread[clayer - 1, c, 3]),
            )
            z2[side, x] = v + flux(diff_ref[...], v, n, parts)

    def finish(x):
        for y in range(8):
            below, above = z2[0, x, y : y + 1, :], z2[1, x, y : y + 1, :]
            v, change = column(v2, 1, x, y, below, above, zcoef(1, x, y), zcoef(4, x, y))
            result[x, y] = 0.5 * v1[2 + x, 2 + y] + 0.5 * (v + change)

    def widen_column(x, y, tile, at):
        for c, value in enumerate(widen(tile, at)):
            spread[2 + x, 2 + y, c] = value

    def widen_layer(clayer, x, tile, at):
        for c, value in enumerate(widen(tile, at)):
            zspread[clayer, 1 + x, c] = value

    def widen_plane(side, places, x, edges, at):
        for i, place_x in enumerate(places):
            tile = kx_in[side, i]
            for y in range(8):
                widen_column(place_x, y, tile, y)
        widen_column(x, -1, ke_in[edges], 7)
        widen_column(x, 8, ke_in[edges + 1], 0)
        widen_layer(1, x, ke_in[4 + edges], at)
        widen_layer(4, x, ke_in[5 + edges], at)

    def widen_sides():
        for side, i, y in ((0, 0, -2), (0, 1, -1), (1, 0, 8), (1, 1, 9)):
            tile = ky_in[side, i]
            for x in range(8):
                widen_column(x, y, tile, x)
        for side, i, clayer in ((0, 0, 0), (0, 1, 1), (1, 0, 4), (1, 1, 5)):
            tile = kz_in[side, i]
            for x in range(8):
                widen_layer(clayer, x, tile, x)
        for i in range(4):
            for c, value in enumerate(widen(kyz_in[i], 0)):
                yzspread[i, c] = value

    def store(i, x, n):
        copy = pltpu.make_async_copy(result.at[pl.ds(x, n)], out.at[pl.ds(x, n)], out_sem.at[i])
        copy.start()
        return copy

    ky[...] = jnp.zeros_like(ky)
    kz[...] = jnp.zeros_like(kz)
    for i in (6, 7, 8):
        loads[i].wait()

    def two_planes(level):
        own_coefficients(2 * level - 2)
        own_coefficients(2 * level - 1)

    chemistry(3, 1, 1, 2, two_planes)
    pl.semaphore_wait(barrier, len(GREETED))
    for steps in AHEAD:
        pl.semaphore_signal(entry_sem, inc=1, device_id=toward(steps), device_id_type=MESH)
    chemistry(3, 1, 3, MAX_SUB, two_planes)
    each(6, 8, lambda x: pack_z(v1, 2, zp, x))
    r_plus = start(send_plus(v1, zp, zf))
    k_plus, k_minus, k_side = send_coefficients()

    loads[5].wait()
    chemistry(0, 3, 1, MAX_SUB)
    each(0, 6, lambda x: pack_z(v1, 2, zp, x))
    pack_yz(v1, 2, yzp)
    r_side = start(send_side(v1, zp, zf, yzp, yz))
    r_minus = send_minus(v1, zp, zf)

    first_along = lax.axis_index("gx") == 0

    def send_back():
        pl.semaphore_wait(entry_sem, len(AHEAD))
        start(k_minus)
        start(r_minus)

    pl.when(jnp.logical_not(first_along))(send_back)

    for copy in k_side:
        copy.wait_recv()
    widen_sides()
    for copy in r_side:
        copy.wait_recv()
    each(1, 7, first_plane)
    each(1, 7, first_rim)
    each(2, 6, finish)
    stored = [store(0, 2, 4)]
    for copy in k_minus:
        copy.wait_recv()
    widen_plane(1, (8, 9), 8, 2, 0)
    for copy in r_minus:
        copy.wait_recv()
    each(7, 9, first_plane)
    first_rim(7)
    each(6, 8, finish)
    stored.append(store(1, 6, 2))

    pl.when(first_along)(send_back)
    for copy in k_plus:
        copy.wait_recv()
    widen_plane(0, (-2, -1), -1, 0, 7)
    for copy in r_plus:
        copy.wait_recv()
    first_plane(-1)
    first_plane(0)
    first_rim(0)
    each(0, 2, finish)
    stored.append(store(2, 0, 2))
    for copy in used:
        copy.wait_send()
    for copy in stored:
        copy.wait()


def shards(sizes, species, substeps, reactants, products, rate_const, velocity, viscosity, diffusivity):
    hbm = pl.BlockSpec(memory_space=pltpu.HBM)
    messages = 36
    return pl.pallas_call(
        functools.partial(kernel, sizes),
        out_shape=jax.ShapeDtypeStruct(species.shape, F32),
        in_specs=[hbm] * 8,
        out_specs=hbm,
        scratch_shapes=[
            pltpu.VMEM((1024, 256), jnp.int32),
            pltpu.VMEM((1024, 256), jnp.int32),
            pltpu.SMEM((4,), jnp.int32),
            pltpu.VMEM((1, 1024), F32),
            pltpu.VMEM((4, 8, 8, 8), F32),
            pltpu.VMEM((1, 256), F32),
            pltpu.VMEM((1024, 512), BF16),
            pltpu.VMEM((1024, 512), BF16),
            pltpu.VMEM((12, 12, 8, 256), F32),
            pltpu.VMEM((10, 10, 8, 256), F32),
            pltpu.VMEM((4, 8, 8, 256), F32),
            pltpu.VMEM((4, 10, 8, 256), F32),
            pltpu.VMEM((4, 8, 256), F32),
            pltpu.VMEM((4, 8, 256), F32),
            pltpu.VMEM((2, 8, 8, 256), F32),
            pltpu.VMEM((8, 8, 8, 128), F32),
            pltpu.VMEM((4, 8, 8, 128), F32),
            pltpu.VMEM((8, 8, 128), F32),
            pltpu.VMEM((8, 8, 128), F32),
            pltpu.VMEM((4, 8, 128), F32),
            pltpu.VMEM((4, 8, 128), F32),
            pltpu.VMEM((2, 2, 8, 128), F32),
            pltpu.VMEM((2, 2, 8, 128), F32),
            pltpu.VMEM((2, 2, 8, 128), F32),
            pltpu.VMEM((8, 8, 128), F32),
            pltpu.VMEM((4, 8, 128), F32),
            pltpu.VMEM((12, 12, 4, 8, 128), F32),
            pltpu.VMEM((6, 10, 4, 8, 128), F32),
            pltpu.VMEM((4, 4, 8, 128), F32),
            pltpu.VMEM((8, 8, 8, 256), F32),
            pltpu.SemaphoreType.DMA((9,)),
            pltpu.SemaphoreType.DMA((3,)),
            pltpu.SemaphoreType.DMA((messages,)),
            pltpu.SemaphoreType.DMA((messages,)),
            pltpu.SemaphoreType.REGULAR,
        ],
        compiler_params=pltpu.CompilerParams(
            collective_id=0, has_side_effects=True, vmem_limit_bytes=63 * 2**20
        ),
    )(
        species,
        reactants,
        products,
        substeps.reshape(-1),
        rate_const.reshape(1, -1),
        velocity,
        viscosity,
        diffusivity.reshape(1, -1),
    )


def solution(mesh):
    return jax.shard_map(
        functools.partial(shards, dict(mesh.shape)),
        mesh=mesh,
        in_specs=(
            P("gx", "gy", "gz", None),
            P("gx", "gy", "gz"),
            P(),
            P(),
            P(),
            P(None, "gx", "gy", "gz"),
            P("gx", "gy", "gz"),
            P(),
        ),
        out_specs=P("gx", "gy", "gz", None),
        check_vma=False,
    )
```

time: 145 us -> 37.8 us (0.26); the launches traced: 143 us -> 37.5 us
  starting transfers between devices: 78.4 us -> 0 us
  Pallas kernels: 0 us -> 35.7 us
  waiting for transfers between devices: 23.7 us -> 0 us
  other arithmetic: 19.9 us -> 0 us
  matrix products: 9.14 us -> 0 us
  local copies, waits for them, and re-layouts: 8.26 us -> 1.87 us
  between operations: 3.04 us -> 0.01 us
    ppermute x18 -> x0, starting transfers between devices: 78.4 us -> none  [the longest x9 52.3 us: with_halo(): after = lax.ppermute(initial, axis, down)]
    pallas_call x0 -> x1, Pallas kernels: none -> 35.7 us  [shards(): pl.pallas_call(functools.partial(kernel, sizes), out_shape=jax.ShapeDtype...]
    ppermute x18 -> x0, waiting for transfers between devices: 23.7 us -> none  [the longest x9 14.3 us: with_halo(): after = lax.ppermute(initial, axis, down)]
    dot_general x12 -> x0, matrix products: 9.14 us -> none  [the longest x6 7.31 us: react(): lax.dot_general(logs, reactant_table, (((1,), (1,)), ((), ())), precision...]
    sort x2 -> x0, other arithmetic: 7.54 us -> none  [the longest x1 3.77 us: integrate(): order = jnp.argsort(-counts)]
    gather x3 -> x0, local copies, waits for them, and re-layouts: 6.64 us -> none  [the longest x1 3.49 us: integrate(): sorted_counts = counts[order]]
    add x2 -> x0, other arithmetic: 5.04 us -> none  [the longest x1 2.9 us: shards(): return 0.5 * field + 0.5 * second]
    another operation x2 -> x0, other arithmetic: 1.77 us -> none
  transfers between devices with their start and end apart: 18 -> 0, of which waited for: 9 -> 0; matrix products, arithmetic and copies ran while one was open for 21% -> 0% of each run, Pallas kernels for 0% -> 0%
where the time goes in v2:
time: 37.8 us; the launch traced here: 37.5 us
  Pallas kernels  35.7 us (94%)
  local copies, waits for them, and re-layouts  1.87 us (5%)
    pallas_call x1, Pallas kernels, shards(): pl.pallas_call(functools.partial(kernel, sizes), out_shape=jax.ShapeDtype...  35.7 us
    unnamed x1, local copies, waits for them, and re-layouts  1.87 us

profile of v2, /device:TPU:1, one launch (start us, length us, event | category | flops | bytes accessed | tf_op | source)
XLA Modules:
  0.0 37.5 jit_solution(10788323328900323523)
XLA Ops:
  0.0 35.7 %shard_map.82 = f32[8,8,8,256]{3,2,1,0:T(8,128)} custom-call(f32[8,8,8,256]{3,2,1,0:T(8,128)} %species.1, s32[1024,256]{1,0:T(8,128)} %reactants.1, s32[1024,256]{1,0:T(8,128)} %products.1, s32[4]{0:T(128)} %bitcast.5, f32[1,1024]{1,0:T(1,128)} %bitcast.3, f32[3,8,8,8]{3,2,1,0:T(8,128)} %velocity.1, f32[8,8,8]{2,1,0:T(8,128)} %viscosity.1, f32[1,256]{1,0:T(1,128)} %bitcast.4), custom_call_target="tpu_custom_call" | custom-call | tf_op jit(solution)/shard_map/pallas_call | solution.py:433
  35.7 1.9 %copy.10 = f32[8,8,8,256]{3,2,1,0:T(8,128)} copy(f32[8,8,8,256]{3,2,1,0:T(8,128)} %shard_map.82) | data formatting | bytes 1048576

commit v3 on v2

--- a/solution.py
+++ b/solution.py
@@ -366,30 +366,39 @@
         own_coefficients(2 * level - 2)
         own_coefficients(2 * level - 1)
 
-    chemistry(3, 1, 1, 2, two_planes)
+    first_along = lax.axis_index("gx") == 0
+    others = jnp.logical_not(first_along)
+
+    def leading(lo, hi):
+        pl.when(first_along)(lambda: chemistry(0, 4, lo, hi, two_planes))
+        pl.when(others)(lambda: chemistry(3, 1, lo, hi, two_planes))
+
+    def remaining():
+        loads[5].wait()
+        chemistry(0, 3, 1, MAX_SUB)
+
+    pl.when(first_along)(loads[5].wait)
+    leading(1, 2)
     pl.semaphore_wait(barrier, len(GREETED))
     for steps in AHEAD:
         pl.semaphore_signal(entry_sem, inc=1, device_id=toward(steps), device_id_type=MESH)
-    chemistry(3, 1, 3, MAX_SUB, two_planes)
+    leading(3, MAX_SUB)
     each(6, 8, lambda x: pack_z(v1, 2, zp, x))
     r_plus = start(send_plus(v1, zp, zf))
     k_plus, k_minus, k_side = send_coefficients()
 
-    loads[5].wait()
-    chemistry(0, 3, 1, MAX_SUB)
+    pl.when(others)(remaining)
     each(0, 6, lambda x: pack_z(v1, 2, zp, x))
     pack_yz(v1, 2, yzp)
     r_side = start(send_side(v1, zp, zf, yzp, yz))
     r_minus = send_minus(v1, zp, zf)
 
-    first_along = lax.axis_index("gx") == 0
-
     def send_back():
         pl.semaphore_wait(entry_sem, len(AHEAD))
         start(k_minus)
         start(r_minus)
 
-    pl.when(jnp.logical_not(first_along))(send_back)
+    pl.when(others)(send_back)
 
     for copy in k_side:
         copy.wait_recv()

time: 37.8 us -> 35.2 us (0.931)
  Pallas kernels: 35.7 us -> 33.1 us
    pallas_call x1, Pallas kernels: 35.7 us -> 33.1 us  [shards(): pl.pallas_call(functools.partial(kernel, sizes), out_shape=jax.ShapeDtype...]
where the time goes in v3:
time: 35.2 us; the launch traced here: 35 us
  Pallas kernels  33.1 us (94%)
  local copies, waits for them, and re-layouts  1.87 us (5%)
    pallas_call x1, Pallas kernels, shards(): pl.pallas_call(functools.partial(kernel, sizes), out_shape=jax.ShapeDtype...  33.1 us
    unnamed x1, local copies, waits for them, and re-layouts  1.87 us

profile of v3, /device:TPU:1, one launch (start us, length us, event | category | flops | bytes accessed | tf_op | source)
XLA Modules:
  0.0 35.0 jit_solution(8812150203575008739)
XLA Ops:
  0.0 33.1 %shard_map.82 = f32[8,8,8,256]{3,2,1,0:T(8,128)} custom-call(f32[8,8,8,256]{3,2,1,0:T(8,128)} %species.1, s32[1024,256]{1,0:T(8,128)} %reactants.1, s32[1024,256]{1,0:T(8,128)} %products.1, s32[4]{0:T(128)} %bitcast.5, f32[1,1024]{1,0:T(1,128)} %bitcast.3, f32[3,8,8,8]{3,2,1,0:T(8,128)} %velocity.1, f32[8,8,8]{2,1,0:T(8,128)} %viscosity.1, f32[1,256]{1,0:T(1,128)} %bitcast.4), custom_call_target="tpu_custom_call" | custom-call | tf_op jit(solution)/shard_map/pallas_call | solution.py:442
  33.2 1.9 %copy.10 = f32[8,8,8,256]{3,2,1,0:T(8,128)} copy(f32[8,8,8,256]{3,2,1,0:T(8,128)} %shard_map.82) | data formatting | bytes 1048576
